TPU v7x, 32 devices: a whole 2x2x4 slice. The times are simulated.
32 devices in a mesh: groups: 2 (over y), pair: 8 (over z, x), aux: 2 (over core).
Axes of the slice: x: 2, y: 2, z: 4, core: 2. Of those that a mesh axis runs over, the one named last changes fastest.
Arguments:
- factors: float32 [8192, 2048], P(('groups', 'pair', 'aux')), parts along dimension 0, may hold values from -0.6 to 0.6
- occupied_energy: float32 [256], P('groups'), parts along dimension 0, may hold values from -3 to -0.4
- virtual_energy: float32 [4096], P('groups'), parts along dimension 0, may hold values from 0.2 to 4
- batch_orbitals: int32 [2], P('groups'), parts along dimension 0, may hold values from 0 to 127, as said below
- panel_order: int32 [32], P('groups'), parts along dimension 0, may hold values from 0 to 31, as said below
Outputs:
- density: float32 [8192, 2048], P(('groups', 'pair', 'aux')), parts along dimension 0
There are 2 independent parts, one for each index of `groups`. A program takes and returns all parts, laid end to end along the dimension named above; each array names one. Nothing has to cross between parts.
Inputs may be any that keep to these rules, and one draw needn't show every extreme that they name: `batch_orbitals`: 1 distinct occupied orbitals. `panel_order`: 16 distinct panel numbers.
All inputs are finite; a program needn't handle non-finite values.
Results may differ from a plain program's by a relative error of at most 0.0001.
Values sent between devices are 32-bit elements; how exact they have to be, the bound alone decides.
A program may use at most 64 MiB of HBM per device.

v0:
```python
import jax
import jax.numpy as jnp
from jax import lax
from jax.sharding import PartitionSpec as P

PANEL = 64
os_scale = 1.3


def spread(block, axis, source):
    block = jnp.where(lax.axis_index(axis) == source, block, jnp.zeros_like(block))
    return lax.psum(block, axis)


def column_energies(columns, batch_energy, virtual_energy):
    nvir = virtual_energy.shape[0]
    nbatch = batch_energy.shape[0]
    orbital = columns // nvir
    virtual = columns % nvir
    occ_part = jnp.sum(
        jnp.where(
            orbital[:, None] == jnp.arange(nbatch, dtype=jnp.int32)[None, :],
            batch_energy[None, :],
            0.0,
        ),
        axis=1,
    )
    vir_part = jnp.sum(
        jnp.where(
            virtual[:, None] == jnp.arange(nvir, dtype=jnp.int32)[None, :],
            virtual_energy[None, :],
            0.0,
        ),
        axis=1,
    )
    return vir_part - occ_part


def batch_energies(occupied_energy, batch_orbitals):
    noccupied = occupied_energy.shape[0]
    return jnp.sum(
        jnp.where(
            batch_orbitals[:, None] == jnp.arange(noccupied, dtype=jnp.int32)[None, :],
            occupied_energy[None, :],
            0.0,
        ),
        axis=1,
    )


def by_columns(factors, occupied_energy, virtual_energy, batch_orbitals, panel_order):
    pair_count = lax.axis_size("pair")
    total_columns = factors.shape[1]
    col_local = total_columns // pair_count
    per_owner = col_local // PANEL
    working = lax.all_to_all(factors, "pair", split_axis=1, concat_axis=0, tiled=True)
    batch_energy = batch_energies(occupied_energy, batch_orbitals)
    own_columns = lax.axis_index("pair") * col_local + jnp.arange(col_local, dtype=jnp.int32)
    own_energy = column_energies(own_columns, batch_energy, virtual_energy)

    def one_panel(position, density):
        number = panel_order[position]
        owner_index = number // per_owner
        panel_slab = lax.dynamic_slice_in_dim(working, number % per_owner * PANEL, PANEL, 1)
        panel_block = spread(panel_slab, "pair", owner_index)
        panel_energy = column_energies(
            number * PANEL + jnp.arange(PANEL, dtype=jnp.int32), batch_energy, virtual_energy
        )
        partial_ints = lax.dot_general(
            panel_block,
            working,
            (((0,), (0,)), ((), ())),
            precision=lax.Precision.HIGHEST,
            preferred_element_type=jnp.float32,
        )
        integrals = lax.psum(partial_ints, "aux")
        amplitudes = os_scale * integrals / (own_energy[None, :] + panel_energy[:, None])
        return density + jnp.dot(
            panel_block,
            amplitudes,
            precision=lax.Precision.HIGHEST,
            preferred_element_type=jnp.float32,
        )

    density = lax.fori_loop(
        0, panel_order.shape[0], one_panel, jnp.zeros(working.shape, jnp.float32)
    )
    return lax.all_to_all(density, "pair", split_axis=0, concat_axis=1, tiled=True)


def by_rows(factors, occupied_energy, virtual_energy, batch_orbitals, panel_order):
    total = factors.shape[1]
    batch_energy = batch_energies(occupied_energy, batch_orbitals)
    nvir = virtual_energy.shape[0]
    energy = (virtual_energy[None, :] - batch_energy[:, None]).reshape(-1)
    panels = jnp.concatenate(
        [
            lax.dynamic_slice_in_dim(factors, panel_order[k] * PANEL, PANEL, 1)
            for k in range(panel_order.shape[0])
        ],
        axis=1,
    )
    chosen = jnp.concatenate(
        [
            lax.dynamic_slice_in_dim(energy, panel_order[k] * PANEL, PANEL, 0)
            for k in range(panel_order.shape[0])
        ]
    )
    partial = lax.dot_general(
        panels,
        factors,
        (((0,), (0,)), ((), ())),
        precision=lax.Precision.HIGH,
        preferred_element_type=jnp.float32,
    )
    mine = lax.psum_scatter(partial, ("pair", "aux"), scatter_dimension=0, tiled=True)
    rank = lax.axis_index("pair") * lax.axis_size("aux") + lax.axis_index("aux")
    my_energy = lax.dynamic_slice_in_dim(chosen, rank * mine.shape[0], mine.shape[0], 0)
    mine = os_scale * mine / (energy[None, :] + my_energy[:, None])
    amplitudes = lax.all_gather(mine, ("pair", "aux"), axis=0, tiled=True)
    return jnp.dot(
        panels, amplitudes, precision=lax.Precision.HIGH, preferred_element_type=jnp.float32
    )


def on_device(factors, occupied_energy, virtual_energy, batch_orbitals, panel_order):
    window = panel_order.shape[0] * PANEL
    fits = 4 * window * factors.shape[1] <= 8 * 1024 * 1024
    plan = by_rows if fits else by_columns
    return plan(factors, occupied_energy, virtual_energy, batch_orbitals, panel_order)


def solution(mesh):
    in_specs = (
        P(("groups", "pair", "aux"), None),
        P("groups"),
        P("groups"),
        P("groups"),
        P("groups"),
    )
    out_specs = P(("groups", "pair", "aux"), None)
    return jax.shard_map(
        on_device, mesh=mesh, in_specs=in_specs, out_specs=out_specs, check_vma=False
    )
```

profile of v0, /device:TPU:0, one launch (start us, length us, event | category | flops | bytes accessed | tf_op | source)
XLA Modules:
  0.0 228.8 jit_solution(1374346407316018232)
XLA Ops:
  6.5 0.0 reduce-scatter.2.cloned.1.call-start
  6.5 2.0 fusion.2
  18.7 3.4 %constant_dynamic-slice_fusion = (f32[256,64]{1,0:T(8,128)S(1)}, f32[256,64]{1,0:T(8,128)S(1)}, f32[256,64]{1,0:T(8,128)S(1)}, f32[256,64]{1,0:T(8,128)}, f32[25...) fusion(f32[256,2048]{1,0:T(8,128)} %param.5, ...), kind=kLoop, calls=%fused_computation.2 | loop fusion | bytes 2097216 | tf_op jit(solution)/shard_map/dynamic_slice | solution.py:98
  22.1 0.0 copy-start
  22.1 1.9 concatenate.6
  24.0 0.3 copy-done
  24.3 5.8 %fusion.3 = f32[1024,2048]{1,0:T(8,128)} fusion(f32[256,1024]{1,0:T(8,128)S(1)} %concatenate.6, f32[256,2048]{1,0:T(8,128)S(1)} %copy-done), kind=kOutput, calls=%fused_computation.22 | convolution fusion | flops 3221225472 | bytes 11534336 | tf_op jit(solution)/shard_map/dot_general | solution.py:109
  30.1 0.0 copy-start.2
  30.1 0.0 copy-start.1
  30.1 0.0 reduce-scatter.2.cloned.1.call-update
  30.1 0.0 all-gather.2.cloned.1.call-start
  30.8 0.0 copy-done.2
  30.8 0.6 fusion
  31.5 0.0 copy-done.1
  31.5 0.6 broadcast_subtract_fusion
  32.1 0.2 fusion.1
  32.3 0.1 concatenate.7
  32.3 0.1 dynamic_slice.131
  32.4 105.1 %reduce-scatter.2.cloned.1.call-done = f32[64,2048]{1,0:T(8,128)} async-done(((f32[1024,2048]{1,0:T(8,128)}), f32[64,2048]{1,0:T(8,128)}) %reduce-scatter.2.cloned.1.call-update) | async-done | bytes 524304 | tf_op jit(solution)/shard_map/reduce_scatter | solution.py:116
  137.6 2.0 add_divide_fusion
  139.6 0.0 all-gather.2.cloned.1.call-update
  139.6 74.8 %all-gather.2.cloned.1.call-done = f32[1024,2048]{1,0:T(8,128)} async-done(((f32[64,2048]{1,0:T(8,128)}), f32[1024,2048]{1,0:T(8,128)}) %all-gather.2.cloned.1.call-update) | async-done | bytes 8388624 | tf_op jit(solution)/shard_map/all_gather | solution.py:120
  214.4 7.6 %fusion.4 = f32[256,2048]{1,0:T(8,128)} fusion(f32[256,1024]{1,0:T(8,128)S(1)} %concatenate.6, f32[1024,2048]{1,0:T(8,128)} %all-gather.2.cloned.1.call-done), kind=kOutput, calls=%fused_computation.23 | convolution fusion | flops 3221225472 | bytes 11534336 | tf_op jit(solution)/shard_map/dot_general | solution.py:121
Async XLA Ops:
  6.5 131.0 %reduce-scatter.2.cloned.1.call-start = ((), (), s32[]{:S(2)}) async-start(), calls=%async_computation.1 | async-start | bytes 8912896 | tf_op jit(solution)/shard_map/reduce_scatter | solution.py:116
  22.1 2.2 copy-start
  30.1 0.7 copy-start.2
  30.1 1.4 copy-start.1
  30.1 184.3 %all-gather.2.cloned.1.call-start = ((), (), s32[]{:S(2)}) async-start(), calls=%async_computation.2 | async-start | bytes 8912896 | tf_op jit(solution)/shard_map/all_gather | solution.py:120
Sparse Core Ops, SparseCore 0:
  30.2 107.2 reduce-scatter.1
  139.7 74.6 all-gather.1
where the time goes:
time: 229 us
  waiting for transfers between devices  180 us (79%)
  between operations  24.3 us (11%)
  matrix products  13.4 us (6%)
  local copies, waits for them, and re-layouts  7.91 us (3%)
  other arithmetic  3.25 us (1%)
    reduce_scatter x1, waiting for transfers between devices, by_rows(): lax.psum_scatter(partial, ('pair', 'aux'), scatter_dimension=0, tiled=True)  105 us
    all_gather x1, waiting for transfers between devices, by_rows(): amplitudes = lax.all_gather(mine, ('pair', 'aux'), axis=0, tiled=True)  74.8 us
    dot_general x1, matrix products, by_rows(): jnp.dot(panels, amplitudes, precision=lax.Precision.HIGH, preferred_eleme...  7.56 us
    dot_general x1, matrix products, by_rows(): lax.dot_general(panels, factors, (((0,), (0,)), ((), ())), precision=lax....  5.8 us
  transfers between devices with their start and end apart: 2, of which 2 were waited for; matrix products, arithmetic and copies ran while one was open for 1% of the time, Pallas kernels for 0%

commit v1 on v0

--- a/solution.py
+++ b/solution.py
@@ -1,3 +1,4 @@
+import functools
 import jax
 import jax.numpy as jnp
 from jax import lax
@@ -5,6 +6,37 @@
 
 PANEL = 64
 os_scale = 1.3
+
+
+def press_wall(own_rows, k_dim):
+    piece_next, raw_out, current_block = (
+        lax.axis_size(("pair", "aux")),
+        lax.axis_index(("pair", "aux")),
+        own_rows.shape[k_dim],
+    )
+    trail = list(map(lambda to_i: (to_i, (to_i + 1) % piece_next), range(piece_next)))
+    in_order = list(map(lambda to_i: (to_i, (to_i - 1) % piece_next), range(piece_next)))
+    lower = jnp.zeros(
+        (*own_rows.shape[:k_dim], piece_next * current_block, *own_rows.shape[k_dim + 1 :]),
+        own_rows.dtype,
+    )
+    lower = lax.dynamic_update_slice_in_dim(lower, own_rows, raw_out * current_block, axis=k_dim)
+    t1 = w1 = own_rows
+    wide_out = piece_next // 2
+    for it in tuple(range(1, wide_out + 1)):
+        t1 = lax.ppermute(t1, ("pair", "aux"), trail)
+        lower = lax.dynamic_update_slice_in_dim(
+            lower, t1, (raw_out - it) % piece_next * current_block, axis=k_dim
+        )
+        if it < piece_next - wide_out:
+            w1 = lax.ppermute(w1, ("pair", "aux"), in_order)
+            lower = lax.dynamic_update_slice_in_dim(
+                lower, w1, (raw_out + it) % piece_next * current_block, axis=k_dim
+            )
+    return lower
+
+
+map_fields_up = functools.partial(press_wall, k_dim=0)
 
 
 def spread(block, axis, source):
@@ -117,7 +149,7 @@
     rank = lax.axis_index("pair") * lax.axis_size("aux") + lax.axis_index("aux")
     my_energy = lax.dynamic_slice_in_dim(chosen, rank * mine.shape[0], mine.shape[0], 0)
     mine = os_scale * mine / (energy[None, :] + my_energy[:, None])
-    amplitudes = lax.all_gather(mine, ("pair", "aux"), axis=0, tiled=True)
+    amplitudes = map_fields_up(mine)
     return jnp.dot(
         panels, amplitudes, precision=lax.Precision.HIGH, preferred_element_type=jnp.float32
     )

time: 229 us -> 264 us (1.15)
  the two profiles are of different devices: /device:TPU:0 before, /device:TPU:10 now
where the time goes in v1:
time: 264 us; the launch traced here: 263 us
  waiting for transfers between devices  182 us (69%)
  local copies, waits for them, and re-layouts  27.6 us (10%)
  between operations  24.7 us (9%)
  matrix products  13.4 us (5%)
  starting transfers between devices  13.1 us (5%)
    reduce_scatter x1, waiting for transfers between devices, by_rows(): lax.psum_scatter(partial, ('pair', 'aux'), scatter_dimension=0, tiled=True)  104 us
    ppermute x8, waiting for transfers between devices, press_wall(): t1 = lax.ppermute(t1, ('pair', 'aux'), trail)  49.8 us
    ppermute x7, waiting for transfers between devices, press_wall(): w1 = lax.ppermute(w1, ('pair', 'aux'), in_order)  28.6 us
    ppermute x7, starting transfers between devices, press_wall(): w1 = lax.ppermute(w1, ('pair', 'aux'), in_order)  13 us
    dynamic_update_slice x7, local copies, waits for them, and re-layouts, press_wall(): lax.dynamic_update_slice_in_dim(lower, w1, (raw_out + it) % piece_next *...  7.94 us
    dynamic_update_slice x8, local copies, waits for them, and re-layouts, press_wall(): lax.dynamic_update_slice_in_dim(lower, t1, (raw_out - it) % piece_next *...  7.78 us
    dot_general x1, matrix products, by_rows(): jnp.dot(panels, amplitudes, precision=lax.Precision.HIGH, preferred_eleme...  7.56 us
    dot_general x1, matrix products, by_rows(): lax.dot_general(panels, factors, (((0,), (0,)), ((), ())), precision=lax....  5.83 us
  transfers between devices with their start and end apart: 16, of which 12 were waited for; matrix products, arithmetic and copies ran while one was open for 6% of the time, Pallas kernels for 0%

profile of v1, /device:TPU:10, one launch (start us, length us, event | category | flops | bytes accessed | tf_op | source)
XLA Modules:
  0.0 263.2 jit_solution(8015272161731179169)
XLA Ops:
  6.5 1.9 fusion.2
  18.7 3.4 %constant_dynamic-slice_fusion = (f32[256,64]{1,0:T(8,128)S(1)}, f32[256,64]{1,0:T(8,128)S(1)}, f32[256,64]{1,0:T(8,128)S(1)}, f32[256,64]{1,0:T(8,128)}, f32[25...) fusion(f32[256,2048]{1,0:T(8,128)} %param.5, ...), kind=kLoop, calls=%fused_computation.17 | loop fusion | bytes 2097216 | tf_op jit(solution)/shard_map/dynamic_slice | solution.py:130
  22.2 1.8 concatenate.6
  24.0 5.8 %fusion.3 = f32[1024,2048]{1,0:T(8,128)} fusion(f32[256,1024]{1,0:T(8,128)S(1)} %concatenate.6, f32[256,2048]{1,0:T(8,128)S(1)} %copy-done), kind=kOutput, calls=%fused_computation.38 | convolution fusion | flops 3221225472 | bytes 11534336 | tf_op jit(solution)/shard_map/dot_general | solution.py:141
  29.8 0.0 reduce-scatter.2.cloned.1.call-update
  30.5 0.6 fusion
  31.2 0.6 broadcast_subtract_fusion
  31.8 0.2 fusion.1
  31.9 0.1 concatenate.7
  32.0 0.1 dynamic_slice.131
  32.1 103.9 %reduce-scatter.2.cloned.1.call-done = f32[64,2048]{1,0:T(8,128)} async-done(((f32[1024,2048]{1,0:T(8,128)}), f32[64,2048]{1,0:T(8,128)}) %reduce-scatter.2.cloned.1.call-update) | async-done | bytes 524304 | tf_op jit(solution)/shard_map/reduce_scatter | solution.py:148
  136.0 4.3 %broadcast_in_dim.6 = f32[1024,2048]{1,0:T(8,128)} broadcast(f32[]{:T(128)} %constant.130.clone.1), dimensions={} | broadcast | bytes 8388612 | tf_op jit(solution)/shard_map/broadcast_in_dim | solution.py:19
  140.3 1.0 constant_dynamic-update-slice_fusion.15
  141.2 1.7 collective-permute-start.1
  143.0 12.5 %collective-permute-done = f32[64,2048]{1,0:T(8,128)S(1)} collective-permute-done((f32[64,2048]{1,0:T(8,128)S(1)}, f32[64,2048]{1,0:T(8,128)S(1)}, u32[]{:S(2)}, u32[]{:S(2)}) %collective-permute-start) | collective-permute-done | bytes 524320 | tf_op jit(solution)/shard_map/ppermute | solution.py:27
  155.5 4.6 %collective-permute-done.1 = f32[64,2048]{1,0:T(8,128)S(1)} collective-permute-done((f32[64,2048]{1,0:T(8,128)S(1)}, f32[64,2048]{1,0:T(8,128)S(1)}, u32[]{:S(2)}, u32[]{:S(2)}) %collective-permute-start.1) | collective-permute-done | bytes 524320 | tf_op jit(solution)/shard_map/ppermute | solution.py:32
  160.0 1.9 collective-permute-start.3
  161.9 6.4 %collective-permute-done.2 = f32[64,2048]{1,0:T(8,128)S(1)} collective-permute-done((f32[64,2048]{1,0:T(8,128)S(1)}, f32[64,2048]{1,0:T(8,128)S(1)}, u32[]{:S(2)}, u32[]{:S(2)}) %collective-permute-start.2) | collective-permute-done | bytes 524320 | tf_op jit(solution)/shard_map/ppermute | solution.py:27
  168.4 10.9 %collective-permute-done.3 = f32[64,2048]{1,0:T(8,128)} collective-permute-done((f32[64,2048]{1,0:T(8,128)S(1)}, f32[64,2048]{1,0:T(8,128)}, u32[]{:S(2)}, u32[]{:S(2)}) %collective-permute-start.3) | collective-permute-done | bytes 524320 | tf_op jit(solution)/shard_map/ppermute | solution.py:32
  179.3 2.0 collective-permute-start.5
  181.3 0.1 collective-permute-start.6
  181.6 1.9 constant_dynamic-update-slice_fusion.14
  183.5 10.4 %collective-permute-done.5 = f32[64,2048]{1,0:T(8,128)S(1)} collective-permute-done((f32[64,2048]{1,0:T(8,128)}, f32[64,2048]{1,0:T(8,128)S(1)}, u32[]{:S(2)}, u32[]{:S(2)}) %collective-permute-start.5) | collective-permute-done | bytes 524320 | tf_op jit(solution)/shard_map/ppermute | solution.py:32
  193.9 1.8 collective-permute-start.7
  195.7 1.9 constant_dynamic-update-slice_fusion.13
  197.6 0.8 constant_dynamic-update-slice_fusion.12
  198.4 1.9 constant_dynamic-update-slice_fusion.11
  200.3 2.1 collective-permute-done.7
  202.4 1.9 collective-permute-start.9
  204.3 0.9 constant_dynamic-update-slice_fusion.10
  205.2 6.6 %collective-permute-done.8 = f32[64,2048]{1,0:T(8,128)S(1)} collective-permute-done((f32[64,2048]{1,0:T(8,128)S(1)}, f32[64,2048]{1,0:T(8,128)S(1)}, u32[]{:S(2)}, u32[]{:S(2)}) %collective-permute-start.8) | collective-permute-done | bytes 524320 | tf_op jit(solution)/shard_map/ppermute | solution.py:27
  211.8 0.8 constant_dynamic-update-slice_fusion.9
  212.6 0.8 constant_dynamic-update-slice_fusion.8
  213.5 0.7 collective-permute-done.9
  214.2 1.9 collective-permute-start.11
  216.1 0.8 constant_dynamic-update-slice_fusion.7
  216.9 8.2 %collective-permute-done.10 = f32[64,2048]{1,0:T(8,128)S(1)} collective-permute-done((f32[64,2048]{1,0:T(8,128)S(1)}, f32[64,2048]{1,0:T(8,128)S(1)}, u32[]{:S(2)}, u32[]{:S(2)}) %collective-permute-start.10) | collective-permute-done | bytes 524320 | tf_op jit(solution)/shard_map/ppermute | solution.py:27
  225.1 0.8 constant_dynamic-update-slice_fusion.6
  226.0 0.8 constant_dynamic-update-slice_fusion.5
  226.8 1.7 collective-permute-start.13
  228.6 0.8 constant_dynamic-update-slice_fusion.4
  229.4 9.9 %collective-permute-done.12 = f32[64,2048]{1,0:T(8,128)S(1)} collective-permute-done((f32[64,2048]{1,0:T(8,128)S(1)}, f32[64,2048]{1,0:T(8,128)S(1)}, u32[]{:S(2)}, u32[]{:S(2)}) %collective-permute-start.12) | collective-permute-done | bytes 524320 | tf_op jit(solution)/shard_map/ppermute | solution.py:27
  239.4 0.8 constant_dynamic-update-slice_fusion.3
  240.2 0.9 constant_dynamic-update-slice_fusion.2
  241.1 0.8 constant_dynamic-update-slice_fusion.1
  241.9 6.1 %collective-permute-done.14 = f32[64,2048]{1,0:T(8,128)S(1)} collective-permute-done((f32[64,2048]{1,0:T(8,128)S(1)}, f32[64,2048]{1,0:T(8,128)S(1)}, u32[]{:S(2)}, u32[]{:S(2)}) %collective-permute-start.14) | collective-permute-done | bytes 524320 | tf_op jit(solution)/shard_map/ppermute | solution.py:27
  248.0 0.8 constant_dynamic-update-slice_fusion
  248.8 7.6 %fusion.4 = f32[256,2048]{1,0:T(8,128)} fusion(f32[256,1024]{1,0:T(8,128)S(1)} %concatenate.6, f32[1024,2048]{1,0:T(8,128)} %constant_dynamic-update-slice_fusion), kind=kOutput, calls=%fused_computation.39 | convolution fusion | flops 3221225472 | bytes 11534336 | tf_op jit(solution)/shard_map/dot_general | solution.py:153
  (24 shorter events, 0.1 us)
Async XLA Ops:
  6.5 17.4 %copy-start = (f32[256,2048]{1,0:T(8,128)S(1)}, f32[256,2048]{1,0:T(8,128)}, u32[]{:S(2)}) copy-start(f32[256,2048]{1,0:T(8,128)} %param.5) | copy-start | bytes 6291460
  6.5 129.4 %reduce-scatter.2.cloned.1.call-start = ((), (), s32[]{:S(2)}) async-start(), calls=%async_computation.1 | async-start | bytes 8912896 | tf_op jit(solution)/shard_map/reduce_scatter | solution.py:148
  24.0 6.5 %copy-start.5 = (f32[128]{0:T(128)S(1)}, f32[128]{0:T(128)}, u32[]{:S(2)}) copy-start(f32[128]{0:T(128)} %param.6) | copy-start | bytes 1540
  24.0 7.2 %copy-start.4 = (f32[2048]{0:T(1024)S(1)}, f32[2048]{0:T(1024)}, u32[]{:S(2)}) copy-start(f32[2048]{0:T(1024)} %param.7) | copy-start | bytes 24580
  136.0 4.3 %copy-start.3 = (f32[64,2048]{1,0:T(8,128)S(1)}, f32[64,2048]{1,0:T(8,128)}, u32[]{:S(2)}) copy-start(f32[64,2048]{1,0:T(8,128)} %reduce-scatter.2.cloned.1.call-done) | copy-start | bytes 1572868
  141.2 14.2 %collective-permute-start = (f32[64,2048]{1,0:T(8,128)S(1)}, f32[64,2048]{1,0:T(8,128)S(1)}, u32[]{:S(2)}, u32[]{:S(2)}) collective-permute-start(f32[64,2048]{1,0:T(8,128)S(1)} %get-tuple-element.6), channel_id=1, source_target_pairs={{0,1},{1,2},{2,3},{3,4},{4,5},{5,6},{6,7},{7,8},{8,9},{9,10},{10,1... | collective-permute-start | bytes 1572872 | tf_op jit(solution)/shard_map/ppermute | solution.py:27
  141.2 18.8 %collective-permute-start.1 = (f32[64,2048]{1,0:T(8,128)S(1)}, f32[64,2048]{1,0:T(8,128)S(1)}, u32[]{:S(2)}, u32[]{:S(2)}) collective-permute-start(f32[64,2048]{1,0:T(8,128)S(1)} %get-tuple-element.6), channel_id=1, source_target_pairs={{0,15},{1,0},{2,1},{3,2},{4,3},{5,4},{6,5},{7,6},{8,7},{9,8},{10,9... | collective-permute-start | bytes 1572872 | tf_op jit(solution)/shard_map/ppermute | solution.py:32
  155.5 25.8 %copy-start.2 = (f32[64,2048]{1,0:T(8,128)}, f32[64,2048]{1,0:T(8,128)S(1)}, u32[]{:S(2)}) copy-start(f32[64,2048]{1,0:T(8,128)S(1)} %collective-permute-done) | copy-start | bytes 1572868
  155.5 12.9 %collective-permute-start.2 = (f32[64,2048]{1,0:T(8,128)S(1)}, f32[64,2048]{1,0:T(8,128)S(1)}, u32[]{:S(2)}, u32[]{:S(2)}) collective-permute-start(f32[64,2048]{1,0:T(8,128)S(1)} %collective-permute-done), channel_id=1, source_target_pairs={{0,1},{1,2},{2,3},{3,4},{4,5},{5,6},{6,7},{7,8},{8,9},{9,10},{10,1... | collective-permute-start | bytes 1572872 | tf_op jit(solution)/shard_map/ppermute | solution.py:27
  160.0 21.2 %copy-start.1 = (f32[64,2048]{1,0:T(8,128)}, f32[64,2048]{1,0:T(8,128)S(1)}, u32[]{:S(2)}) copy-start(f32[64,2048]{1,0:T(8,128)S(1)} %collective-permute-done.1) | copy-start | bytes 1572868
  160.0 19.2 %collective-permute-start.3 = (f32[64,2048]{1,0:T(8,128)S(1)}, f32[64,2048]{1,0:T(8,128)}, u32[]{:S(2)}, u32[]{:S(2)}) collective-permute-start(f32[64,2048]{1,0:T(8,128)S(1)} %collective-permute-done.1), channel_id=1, source_target_pairs={{0,15},{1,0},{2,1},{3,2},{4,3},{5,4},{6,5},{7,6},{8,7},{9,8},{10,9... | collective-permute-start | bytes 1572872 | tf_op jit(solution)/shard_map/ppermute | solution.py:32
  168.4 12.9 %collective-permute-start.4 = (f32[64,2048]{1,0:T(8,128)S(1)}, f32[64,2048]{1,0:T(8,128)S(1)}, u32[]{:S(2)}, u32[]{:S(2)}) collective-permute-start(f32[64,2048]{1,0:T(8,128)S(1)} %collective-permute-done.2), channel_id=1, source_target_pairs={{0,1},{1,2},{2,3},{3,4},{4,5},{5,6},{6,7},{7,8},{8,9},{9,10},{10,1... | collective-permute-start | bytes 1572872 | tf_op jit(solution)/shard_map/ppermute | solution.py:27
  179.3 14.6 %collective-permute-start.5 = (f32[64,2048]{1,0:T(8,128)}, f32[64,2048]{1,0:T(8,128)S(1)}, u32[]{:S(2)}, u32[]{:S(2)}) collective-permute-start(f32[64,2048]{1,0:T(8,128)} %collective-permute-done.3), channel_id=1, source_target_pairs={{0,15},{1,0},{2,1},{3,2},{4,3},{5,4},{6,5},{7,6},{8,7},{9,8},{10,9... | collective-permute-start | bytes 1572872 | tf_op jit(solution)/shard_map/ppermute | solution.py:32
  181.3 16.3 %collective-permute-start.6 = (f32[64,2048]{1,0:T(8,128)S(1)}, f32[64,2048]{1,0:T(8,128)S(1)}, u32[]{:S(2)}, u32[]{:S(2)}) collective-permute-start(f32[64,2048]{1,0:T(8,128)S(1)} %collective-permute-done.4), channel_id=1, source_target_pairs={{0,1},{1,2},{2,3},{3,4},{4,5},{5,6},{6,7},{7,8},{8,9},{9,10},{10,1... | collective-permute-start | bytes 1572872 | tf_op jit(solution)/shard_map/ppermute | solution.py:27
  193.9 8.5 %collective-permute-start.7 = (f32[64,2048]{1,0:T(8,128)S(1)}, f32[64,2048]{1,0:T(8,128)S(1)}, u32[]{:S(2)}, u32[]{:S(2)}) collective-permute-start(f32[64,2048]{1,0:T(8,128)S(1)} %collective-permute-done.5), channel_id=1, source_target_pairs={{0,15},{1,0},{2,1},{3,2},{4,3},{5,4},{6,5},{7,6},{8,7},{9,8},{10,9... | collective-permute-start | bytes 1572872 | tf_op jit(solution)/shard_map/ppermute | solution.py:32
  197.6 14.2 %collective-permute-start.8 = (f32[64,2048]{1,0:T(8,128)S(1)}, f32[64,2048]{1,0:T(8,128)S(1)}, u32[]{:S(2)}, u32[]{:S(2)}) collective-permute-start(f32[64,2048]{1,0:T(8,128)S(1)} %collective-permute-done.6), channel_id=1, source_target_pairs={{0,1},{1,2},{2,3},{3,4},{4,5},{5,6},{6,7},{7,8},{8,9},{9,10},{10,1... | collective-permute-start | bytes 1572872 | tf_op jit(solution)/shard_map/ppermute | solution.py:27
  202.4 11.8 %collective-permute-start.9 = (f32[64,2048]{1,0:T(8,128)S(1)}, f32[64,2048]{1,0:T(8,128)S(1)}, u32[]{:S(2)}, u32[]{:S(2)}) collective-permute-start(f32[64,2048]{1,0:T(8,128)S(1)} %collective-permute-done.7), channel_id=1, source_target_pairs={{0,15},{1,0},{2,1},{3,2},{4,3},{5,4},{6,5},{7,6},{8,7},{9,8},{10,9... | collective-permute-start | bytes 1572872 | tf_op jit(solution)/shard_map/ppermute | solution.py:32
  211.8 13.3 %collective-permute-start.10 = (f32[64,2048]{1,0:T(8,128)S(1)}, f32[64,2048]{1,0:T(8,128)S(1)}, u32[]{:S(2)}, u32[]{:S(2)}) collective-permute-start(f32[64,2048]{1,0:T(8,128)S(1)} %collective-permute-done.8), channel_id=1, source_target_pairs={{0,1},{1,2},{2,3},{3,4},{4,5},{5,6},{6,7},{7,8},{8,9},{9,10},{10,1... | collective-permute-start | bytes 1572872 | tf_op jit(solution)/shard_map/ppermute | solution.py:27
  214.2 12.6 %collective-permute-start.11 = (f32[64,2048]{1,0:T(8,128)S(1)}, f32[64,2048]{1,0:T(8,128)S(1)}, u32[]{:S(2)}, u32[]{:S(2)}) collective-permute-start(f32[64,2048]{1,0:T(8,128)S(1)} %collective-permute-done.9), channel_id=1, source_target_pairs={{0,15},{1,0},{2,1},{3,2},{4,3},{5,4},{6,5},{7,6},{8,7},{9,8},{10,9... | collective-permute-start | bytes 1572872 | tf_op jit(solution)/shard_map/ppermute | solution.py:32
  225.1 14.2 %collective-permute-start.12 = (f32[64,2048]{1,0:T(8,128)S(1)}, f32[64,2048]{1,0:T(8,128)S(1)}, u32[]{:S(2)}, u32[]{:S(2)}) collective-permute-start(f32[64,2048]{1,0:T(8,128)S(1)} %collective-permute-done.10), channel_id=1, source_target_pairs={{0,1},{1,2},{2,3},{3,4},{4,5},{5,6},{6,7},{7,8},{8,9},{9,10},{10,1... | collective-permute-start | bytes 1572872 | tf_op jit(solution)/shard_map/ppermute | solution.py:27
  226.8 14.3 %collective-permute-start.13 = (f32[64,2048]{1,0:T(8,128)S(1)}, f32[64,2048]{1,0:T(8,128)S(1)}, u32[]{:S(2)}, u32[]{:S(2)}) collective-permute-start(f32[64,2048]{1,0:T(8,128)S(1)} %collective-permute-done.11), channel_id=1, source_target_pairs={{0,15},{1,0},{2,1},{3,2},{4,3},{5,4},{6,5},{7,6},{8,7},{9,8},{10,9... | collective-permute-start | bytes 1572872 | tf_op jit(solution)/shard_map/ppermute | solution.py:32
  239.3 8.6 %collective-permute-start.14 = (f32[64,2048]{1,0:T(8,128)S(1)}, f32[64,2048]{1,0:T(8,128)S(1)}, u32[]{:S(2)}, u32[]{:S(2)}) collective-permute-start(f32[64,2048]{1,0:T(8,128)S(1)} %collective-permute-done.12), channel_id=1, source_target_pairs={{0,1},{1,2},{2,3},{3,4},{4,5},{5,6},{6,7},{7,8},{8,9},{9,10},{10,1... | collective-permute-start | bytes 1572872 | tf_op jit(solution)/shard_map/ppermute | solution.py:27
Sparse Core Ops, SparseCore 0:
  30.0 105.9 reduce-scatter.1
